TPU v7x, 512 devices: a whole 4x4x16 slice. The times are simulated.
512 devices in a mesh: pair: 64 (over y, z), ints: 8 (over x, core).
Axes of the slice: x: 4, y: 4, z: 16, core: 2. Of those that a mesh axis runs over, the one named last changes fastest.
Arguments:
- amp_tiles: bfloat16 [1536, 128, 128], P('pair'), may hold values from -6 to 6
- amp_row: int32 [64, 24], replicated, may hold values from 0 to 1
- amp_col: int32 [64, 24], replicated, may hold values from 0 to 23
- amp_dest: int32 [64, 24], replicated, may hold values from 0 to 127, as said below
- amp_count: int32 [64], replicated, may hold values from 12 to 24, as said below
- ladder_ints: bfloat16 [3072, 3072], P('pair', 'ints'), may hold values from -0.21875 to 0.21875
- ladder_present: int32 [24, 24], P(None, 'ints'), may hold values 0 or 1
- cycle_ints: bfloat16 [3072, 3072], P('pair', 'ints'), may hold values from -0.21875 to 0.21875
- cycle_present: int32 [24, 24], P(None, 'ints'), may hold values 0 or 1
Outputs:
- ladder: bfloat16 [16384, 3072], P('pair', 'ints')
- cycle: bfloat16 [16384, 3072], P('pair', 'ints')
Inputs may be any that keep to these rules, and one draw needn't show every extreme that they name: On each pair device, amp_dest // 2 names every pair device at most 2 times over the 24 slots, and some device exactly 2 times. `amp_count`: some pair device uses all 24 slots.
All inputs are finite; a program needn't handle non-finite values. No bound on the sum of `ladder_present` or of `cycle_present` on one device may be relied on, other than what follows from the above.
Results may differ from a plain program's by a relative error of at most 0.0041.
Values may be sent and summed in bfloat16 or wider, within the bound.
A program may use at most 64 MiB of HBM per device.

v0:
```python
import jax
import jax.numpy as jnp
from jax import lax
from jax.sharding import PartitionSpec as P

TILE = 128
RT_DEV = 2


def place(tiles, index, width):
    grid = jnp.zeros((RT_DEV * width, TILE, TILE), jnp.float32)
    grid = grid.at[index].add(tiles.astype(jnp.float32))
    grid = grid.reshape(RT_DEV, width, TILE, TILE).transpose(0, 2, 1, 3)
    return grid.reshape(RT_DEV * TILE, width * TILE).astype(jnp.bfloat16)


def expand_rows(present):
    rows = jnp.repeat(present, TILE, axis=0)
    return jnp.repeat(rows, TILE, axis=1).astype(jnp.bfloat16)


def contract(dense, present, piece):
    keep = expand_rows(present)
    return jnp.dot(dense, piece * keep, preferred_element_type=jnp.float32)


def shards(
    amp_tiles,
    amp_row,
    amp_col,
    amp_dest,
    amp_count,
    ladder_ints,
    ladder_present,
    cycle_ints,
    cycle_present,
):
    here = lax.axis_index("pair")
    peers = lax.axis_size("pair")
    slots = amp_tiles.shape[0]
    width = ladder_present.shape[0]
    capacity = 2 * ((slots + 2 * peers - 1) // (2 * peers))
    active_all = (jnp.arange(slots)[None, :] < amp_count[:, None]).astype(jnp.int32)
    mine = lax.dynamic_index_in_dim(active_all, here, 0, keepdims=False)
    my_row = lax.dynamic_index_in_dim(amp_row, here, 0, keepdims=False)
    my_col = lax.dynamic_index_in_dim(amp_col, here, 0, keepdims=False)
    live = amp_tiles * mine.astype(jnp.bfloat16)[:, None, None]
    amp_dense = place(live, my_row * width + my_col, width)
    owner = amp_dest // RT_DEV
    my_owner = lax.dynamic_index_in_dim(owner, here, 0, keepdims=False)
    bucket_ids = jnp.arange(capacity)[None, :, None]
    target = jnp.arange(peers)[:, None] == my_owner[None, :]
    rank = jnp.cumsum(target.astype(jnp.int32), axis=1) - 1
    pick = (target[:, None, :] & (rank[:, None, :] == bucket_ids)).astype(jnp.int32)
    which = jnp.sum(pick * jnp.arange(slots)[None, None, :], axis=2)
    filled = jnp.sum(pick, axis=2)
    outgoing = live[which] * filled.astype(jnp.bfloat16)[:, :, None, None]
    arrive = owner == here
    rank_in = jnp.cumsum(arrive.astype(jnp.int32), axis=1) - 1
    pick_in = (arrive[:, None, :] & (rank_in[:, None, :] == bucket_ids)).astype(jnp.int32)
    in_row = jnp.sum(pick_in * (amp_dest % RT_DEV)[:, None, :], axis=2)
    in_col = jnp.sum(pick_in * amp_col[:, None, :], axis=2)
    index_in = (in_row * width + in_col).reshape(-1)
    incoming = lax.all_to_all(outgoing, "pair", split_axis=0, concat_axis=0, tiled=True)
    flipped = jnp.swapaxes(incoming, 2, 3).reshape(peers * capacity, TILE, TILE)
    ladder = contract(
        amp_dense, ladder_present, lax.all_gather(ladder_ints, "pair", axis=0, tiled=True)
    )
    cycle_dense = place(flipped, index_in, width)
    cycle = contract(
        cycle_dense, cycle_present, lax.all_gather(cycle_ints, "pair", axis=0, tiled=True)
    )
    return (ladder.astype(jnp.bfloat16), cycle.astype(jnp.bfloat16))


def solution(mesh):
    placed = (
        P("pair", None, None),
        P(),
        P(),
        P(),
        P(),
        P("pair", "ints"),
        P(None, "ints"),
        P("pair", "ints"),
        P(None, "ints"),
    )
    return jax.shard_map(
        shards,
        mesh=mesh,
        in_specs=placed,
        out_specs=(P("pair", "ints"), P("pair", "ints")),
        check_vma=False,
    )
```

profile of v0, /device:TPU:2, one launch (start us, length us, event | category | flops | bytes accessed | tf_op | source)
XLA Modules:
  0.0 435.9 jit_solution(13417465527615851472)
XLA Ops:
  7.2 0.8 copy.43
  8.0 0.2 reduce_window_sum.18
  8.2 0.1 copy.52
  8.3 0.1 copy.51
  8.4 0.1 copy.53
  8.5 0.1 reshape.167
  8.7 1.2 dynamic-slice
  9.9 0.6 fusion.18
  10.6 0.1 copy.54
  10.7 2.5 fusion.23
  13.2 3.1 gather_fusion
  16.3 4.5 %broadcast_multiply_fusion = bf16[64,2,128,128]{3,2,1,0:T(8,128)(2,1)} fusion(bf16[64,2,128,128]{3,2,1,0:T(8,128)(2,1)} %bitcast.57, bf16[64,2]{1,0:T(8,128)(2,1)S(1)} %copy.54), kind=kLoop, calls=%fused_computation.6 | loop fusion | flops 2097152 | bytes 8388864 | tf_op jit(solution)/shard_map/mul | solution.py:57
  20.7 19.1 %all-to-all-start = ((bf16[64,2,128,128]{3,2,1,0:T(8,128)(2,1)}), bf16[64,2,128,128]{3,2,1,0:T(8,128)(2,1)}, u32[]{:S(2)}, u32[]{:S(2)}) async-start(bf16[64,2,128,128]{3,2,1,0:T(8,128)(2,1)} %broadcast_multiply_fusion), calls=%async_computation | async-start | bytes 8388608 | tf_op jit(solution)/shard_map/all_to_all | solution.py:64
  39.9 0.0 all-gather.5.cloned.1.call-start
  39.9 0.7 all-gather.5.cloned.1.call-update
  40.6 0.0 all-gather.3.cloned.1.call-start
  40.7 0.7 all-gather.3.cloned.1.call-update
  41.4 0.2 reduce_window_sum.17
  41.6 0.1 copy.48
  41.6 0.1 copy.47
  41.7 0.1 copy.49
  41.9 0.1 copy.50
  42.0 0.1 add.94
  42.1 0.1 broadcast_bitcast_fusion
  42.2 0.2 add_reduce_fusion
  42.4 0.4 broadcast.131.clone
  42.8 4.5 %scatter_fusion = f32[48,128,128]{2,1,0:T(8,128)S(1)} fusion(f32[48,128,128]{2,1,0:T(8,128)S(1)} %broadcast.131.clone, s32[24]{0:T(128)S(1)} %fusion.19, f32[24,128,128]{2,1,0:T(8,128)} %get-tuple-element.9), kind=kCustom, calls=%fused_computation.1 | custom fusion | flops 393216 | bytes 4718688 | tf_op jit(solution)/shard_map/scatter-add | solution.py:12
  47.3 0.3 convert_element_type.102
  47.6 0.0 copy-start.5
  47.6 2.2 copy.41
  49.7 0.1 broadcast_bitcast_fusion.1
  49.9 188.7 %all-gather.5.cloned.1.call-done = bf16[3072,384]{1,0:T(8,128)(2,1)} async-done(((bf16[48,384]{1,0:T(8,128)(2,1)}), bf16[3072,384]{1,0:T(8,128)(2,1)}) %all-gather.5.cloned.1.call-update) | async-done | bytes 2359312 | tf_op jit(solution)/shard_map/all_gather | solution.py:71
  238.6 2.8 copy.57
  241.4 1.6 bitcast_multiply_fusion
  243.0 143.6 %all-gather.3.cloned.1.call-done = bf16[3072,384]{1,0:T(8,128)(2,1)} async-done(((bf16[48,384]{1,0:T(8,128)(2,1)}), bf16[3072,384]{1,0:T(8,128)(2,1)}) %all-gather.3.cloned.1.call-update) | async-done | bytes 2359312 | tf_op jit(solution)/shard_map/all_gather | solution.py:67
  386.6 2.8 copy.42
  389.5 0.2 bitcast_multiply_fusion.1
  389.7 1.2 copy-done.1
  390.9 1.7 fusion.6
  392.6 0.0 all-to-all-done
  392.6 6.5 %convert_bitcast_fusion = f32[64,2,128,128]{2,3,1,0:T(8,128)} fusion(bf16[64,2,128,128]{3,2,1,0:T(8,128)(2,1)} %all-to-all-done), kind=kLoop, calls=%fused_computation.3 | loop fusion | flops 2097152 | bytes 12582912 | tf_op jit(solution)/shard_map/convert_element_type | solution.py:12
  399.1 9.0 %copy.55 = f32[64,2,128,128]{3,2,1,0:T(8,128)} copy(f32[64,2,128,128]{2,3,1,0:T(8,128)} %convert_bitcast_fusion) | data formatting | bytes 16777216 | tf_op jit(solution)/shard_map/convert_element_type | solution.py:12
  408.1 0.4 broadcast.131.clone.1
  408.4 17.0 %scatter_fusion.1 = f32[48,128,128]{2,1,0:T(8,128)S(1)} fusion(f32[48,128,128]{2,1,0:T(8,128)S(1)} %broadcast.131.clone.1, s32[128]{0:T(128)S(1)} %fusion.20, f32[128,128,128]{2,1,0:T(8,128)} %bitcast.56), kind=kCustom, calls=%fused_computation.2 | custom fusion | flops 2097152 | bytes 25166336 | tf_op jit(solution)/shard_map/scatter-add | solution.py:12
  425.5 0.3 convert_element_type.117
  425.7 1.0 copy.56
  426.8 0.6 copy-done
  427.4 1.7 fusion.9
  (27 shorter events, 0.3 us)
Async XLA Ops:
  20.7 21.1 %copy-start.2 = (s32[64,24]{0,1:T(8,128)S(1)}, s32[64,24]{0,1:T(8,128)}, u32[]{:S(2)}) copy-start(s32[64,24]{0,1:T(8,128)} %param.11) | copy-start | bytes 18436
  20.7 21.4 %copy-start.4 = (s32[24,3]{0,1:T(4,128)S(1)}, s32[24,3]{0,1:T(4,128)}, u32[]{:S(2)}) copy-start(s32[24,3]{0,1:T(4,128)} %param.17) | copy-start | bytes 868
  20.7 21.5 %copy-start.3 = (s32[64,24]{0,1:T(8,128)S(1)}, s32[64,24]{0,1:T(8,128)}, u32[]{:S(2)}) copy-start(s32[64,24]{0,1:T(8,128)} %param.10) | copy-start | bytes 18436
  20.7 371.8 %all-to-all-start = ((bf16[64,2,128,128]{3,2,1,0:T(8,128)(2,1)}), bf16[64,2,128,128]{3,2,1,0:T(8,128)(2,1)}, u32[]{:S(2)}, u32[]{:S(2)}) async-start(bf16[64,2,128,128]{3,2,1,0:T(8,128)(2,1)} %broadcast_multiply_fusion), calls=%async_computation | async-start | bytes 8388608 | tf_op jit(solution)/shard_map/all_to_all | solution.py:64
  39.9 198.7 %all-gather.5.cloned.1.call-start = ((), (), s32[]{:S(2)}) async-start(), calls=%async_computation.2 | async-start | bytes 2396160 | tf_op jit(solution)/shard_map/all_gather | solution.py:71
  40.6 346.0 %all-gather.3.cloned.1.call-start = ((), (), s32[]{:S(2)}) async-start(), calls=%async_computation.1 | async-start | bytes 2396160 | tf_op jit(solution)/shard_map/all_gather | solution.py:67
  47.6 2.2 copy-start.5
  389.5 1.4 copy-start.1
  425.7 1.7 copy-start
Sparse Core Ops, SparseCore 0:
  43.7 194.8 all-gather.4
  241.6 145.0 all-gather.2
where the time goes:
time: 437 us; the launch traced here: 436 us
  waiting for transfers between devices  334 us (76%)
  other arithmetic  38.6 us (9%)
  local copies, waits for them, and re-layouts  26.7 us (6%)
  starting transfers between devices  19.2 us (4%)
  between operations  14.3 us (3%)
    all_gather x1, waiting for transfers between devices, shards(): lax.all_gather(cycle_ints, 'pair', axis=0, tiled=True)  189 us
    all_gather x1, waiting for transfers between devices, shards(): lax.all_gather(ladder_ints, 'pair', axis=0, tiled=True)  144 us
    scatter-add x2, other arithmetic, place(): grid = grid.at[index].add(tiles.astype(jnp.float32))  21.5 us
    all_to_all x1, starting transfers between devices, shards(): lax.all_to_all(outgoing, 'pair', split_axis=0, concat_axis=0, tiled=True)  19.1 us
    convert_element_type x1, local copies, waits for them, and re-layouts, place(): grid = grid.at[index].add(tiles.astype(jnp.float32))  9.01 us
    convert_element_type x2, other arithmetic, place(): grid = grid.at[index].add(tiles.astype(jnp.float32))  9 us
  transfers between devices with their start and end apart: 3, of which 2 were waited for; matrix products, arithmetic and copies ran while one was open for 4% of the time, Pallas kernels for 0%

commit v1 on v0

v1 whole, which is shorter than its diff:
```python
import jax
import jax.numpy as jnp
from jax import lax
from jax.experimental import pallas as pl
from jax.experimental.pallas import tpu as pltpu
from jax.sharding import PartitionSpec as P

TILE = 128
NCT = 24
SLOTS = 24
NY = 4
NZ = 16
NX = 4
PART = 16
ROWS = 48
COLS = 384
HALF = NZ // 2
MESH = pl.DeviceIdType.MESH
F32 = jnp.float32
BF16 = jnp.bfloat16


def kernel(
    lp, cp, sel, order, cont, last, some, a_order, a_cont, a_last, a_some,
    wl, wr, tiles,
    out_l, out_c,
    w, t, ysend, yrecv, pre, bt, a_src, a_pre, a, acc,
    loc, zw_s, zw_r, zt_s, zt_r, y1_s, y1_r, y2_s, y2_r, ya_s, ya_r, xs_s, xs_r, co_s, co_r,
):
    p = lax.axis_index("pair")
    i = lax.axis_index("ints")
    y, z = p // NZ, p % NZ
    x, core = i // 2, i % 2

    def at(yy, zz):
        return (lax.rem(yy + NY, NY) * NZ + lax.rem(zz + NZ, NZ), i)

    def at_x(xx):
        return (p, lax.rem(xx + NX, NX) * 2 + core)

    zn = (at(y, z + 1), at(y, z - 1))
    yn = (at(y + 1, z), at(y - 1, z))
    xn = (at_x(x + 1), at_x(x - 1))
    twin = (p, x * 2 + 1 - core)

    tile_here = pltpu.make_async_copy(
        tiles.at[:, pl.ds(pl.multiple_of(PART * i, PART), PART), :],
        t.at[pl.ds(z * SLOTS, SLOTS)], loc.at[0])
    tile_here.start()
    tile_all = pltpu.make_async_copy(tiles, a_src, loc.at[1])
    tile_all.start()

    barrier = pltpu.get_barrier_semaphore()
    greet = (*zn, *yn, at(y + 2, z), *xn, twin)
    for dev in greet:
        pl.semaphore_signal(barrier, inc=1, device_id=dev, device_id_type=MESH)

    for k, (src, present) in enumerate(((wl, lp), (wr, cp))):
        for g in range(ROWS // PART):
            row = (3 * p + g) // 8
            for n in range(COLS // TILE):
                keep = present[row * 3 + n].astype(F32)
                block = src[g * PART:(g + 1) * PART, n * TILE:(n + 1) * TILE].astype(F32)
                w[k, pl.ds(pl.multiple_of(ROWS * p + g * PART, PART), PART), n * TILE:(n + 1) * TILE] = (
                    block * keep).astype(BF16)
    tile_here.wait()
    pl.semaphore_wait(barrier, len(greet))

    sends = []

    def send(src, dst, ss, rs, dev):
        c = pltpu.make_async_remote_copy(
            src_ref=src, dst_ref=dst, send_sem=ss, recv_sem=rs, device_id=dev, device_id_type=MESH)
        c.start()
        sends.append(c)

    def arrived(buf, ss, rs, dev):
        pltpu.make_async_remote_copy(
            src_ref=buf, dst_ref=buf, send_sem=ss, recv_sem=rs, device_id=dev, device_id_type=MESH).wait_recv()

    def w_at(yy, zz, part=None):
        q = lax.rem(yy + NY, NY) * NZ + lax.rem(zz + NZ, NZ)
        rows = pl.ds(pl.multiple_of(q * ROWS, PART), ROWS)
        if part is None:
            return w.at[:, rows, :]
        return w.at[part, rows, :]

    def t_at(zz, part=None):
        q = lax.rem(zz + NZ, NZ)
        if part is None:
            return t.at[pl.ds(q * SLOTS, SLOTS)]
        return t.at[pl.ds(q * SLOTS + part * (SLOTS // 2), SLOTS // 2)]

    def y_forward(zz, j):
        for d in range(2):
            send(w_at(y, zz), w_at(y, zz), y1_s.at[d, j], y1_r.at[d, j], yn[d])

    def place_a(j, run):
        run = a_src[a_order[j]].astype(F32) + a_cont[j] * run
        a_pre[j] = run
        return run

    y_forward(z, 0)
    for s in range(HALF):
        for d in range(2):
            zz = z - s if d == 0 else z + s
            part = d if s == HALF - 1 else None
            send(w_at(y, zz, part), w_at(y, zz, part), zw_s.at[d, s], zw_r.at[d, s], zn[d])
            send(t_at(zz, part), t_at(zz, part), zt_s.at[d, s], zt_r.at[d, s], zn[d])
        if s == 0:
            tile_all.wait()
            lax.fori_loop(0, SLOTS, place_a, jnp.zeros((TILE, TILE), F32))
        if s in (1, 2):
            r = s - 1
            for c in range(NCT):
                a[r * TILE:(r + 1) * TILE, c * TILE:(c + 1) * TILE] = (
                    a_pre[a_last[r * NCT + c]] * a_some[r * NCT + c]).astype(BF16)
        for d in range(2):
            zz = z - s - 1 if d == 0 else z + s + 1
            part = d if s == HALF - 1 else None
            arrived(w_at(y, zz, part), zw_s.at[d, s], zw_r.at[d, s], zn[d])
            if s < HALF - 1:
                y_forward(zz, 2 * s + 1 + d)
        if s == HALF - 1:
            y_forward(z - HALF, NZ - 1)
        for d in range(2):
            zz = z - s - 1 if d == 0 else z + s + 1
            part = d if s == HALF - 1 else None
            arrived(t_at(zz, part), zt_s.at[d, s], zt_r.at[d, s], zn[d])

    for dy in (1, 2, 3, 0):
        first = lax.rem(y + dy, NY) * 32

        def choose(j, _, dy=dy, first=first):
            tile = t[sel[first + j]]
            if dy == 0:
                yrecv[y * 32 + j] = tile
            else:
                ysend[(dy - 1) * 32 + j] = tile
            return 0

        lax.fori_loop(0, 32, choose, 0, unroll=8)
        if dy > 0:
            send(ysend.at[pl.ds((dy - 1) * 32, 32)], yrecv.at[pl.ds(y * 32, 32)],
                 ya_s.at[dy - 1], ya_r.at[dy - 1], at(y + dy, z))

    def step_z(j):
        if j == 0:
            return z
        if j == NZ - 1:
            return z - HALF
        s = (j + 1) // 2
        return z - s if j % 2 == 1 else z + s

    for j in range(NZ):
        zz = step_z(j)
        for d in range(2):
            yy = y - 1 if d == 0 else y + 1
            arrived(w_at(yy, zz), y1_s.at[d, j], y1_r.at[d, j], yn[d])
            send(w_at(yy, zz, d), w_at(yy, zz, d), y2_s.at[d, j], y2_r.at[d, j], yn[d])

    for dy in (1, 2, 3):
        yy = lax.rem(y - dy + NY, NY)
        arrived(yrecv.at[pl.ds(yy * 32, 32)], ya_s.at[dy - 1], ya_r.at[dy - 1], at(y + dy, z))

    def add_up(j, run):
        run = yrecv[order[j]].astype(F32) + cont[j] * run
        pre[j] = run
        return run

    lax.fori_loop(0, 128, add_up, jnp.zeros((PART, TILE), F32), unroll=8)

    def bt_at(ii, lo=0, num=NCT):
        return bt.at[pl.ds(lo, num), pl.ds(pl.multiple_of(ii * PART, PART), PART), :]

    for q in range(2 * NCT):
        c, r = q // 2, q % 2
        bt[c, pl.ds(pl.multiple_of(i * PART, PART), PART), r * TILE:(r + 1) * TILE] = (
            pre[last[q]] * some[q]).astype(BF16)

    for d in range(2):
        send(bt_at(i), bt_at(i), xs_s.at[d], xs_r.at[d], xn[d])
    send(bt_at(i), bt_at(i), co_s.at[0], co_r.at[0], twin)
    half = NCT // 2
    for d in range(2):
        ii = xn[1 - d][1]
        arrived(bt_at(ii), xs_s.at[d], xs_r.at[d], xn[d])
        send(bt_at(ii, d * half, half), bt_at(ii, d * half, half), xs_s.at[2 + d], xs_r.at[2 + d], xn[d])
        send(bt_at(ii), bt_at(ii), co_s.at[1 + d], co_r.at[1 + d], twin)
    far = at_x(x + 2)[1]
    for d in range(2):
        arrived(bt_at(far, d * half, half), xs_s.at[2 + d], xs_r.at[2 + d], xn[d])
        send(bt_at(far, d * half, half), bt_at(far, d * half, half), co_s.at[3 + d], co_r.at[3 + d], twin)

    for j in range(NZ):
        zz = step_z(j)
        for d in range(2):
            arrived(w_at(y + 2, zz, d), y2_s.at[d, j], y2_r.at[d, j], yn[d])

    depth = 512
    acc[...] = jnp.zeros_like(acc)

    @pl.loop(0, NCT * TILE // depth)
    def _(k):
        cut = pl.ds(pl.multiple_of(k * depth, depth), depth)
        acc[...] += jnp.dot(a[:, cut], w[0, cut, :], preferred_element_type=F32)

    out_l[...] = acc[...].astype(BF16)

    def other(ii):
        return lax.div(ii, 2) * 2 + 1 - lax.rem(ii, 2)

    arrived(bt_at(other(i)), co_s.at[0], co_r.at[0], twin)
    for d in range(2):
        arrived(bt_at(other(xn[1 - d][1])), co_s.at[1 + d], co_r.at[1 + d], twin)
    for d in range(2):
        arrived(bt_at(other(far), d * half, half), co_s.at[3 + d], co_r.at[3 + d], twin)

    acc[...] = jnp.zeros_like(acc)

    @pl.loop(0, NCT * TILE // depth)
    def _(k):
        cut = pl.ds(pl.multiple_of(k * depth, depth), depth)
        part = bt[pl.ds(k * (depth // TILE), depth // TILE)].reshape(depth, 2 * TILE)
        acc[...] += lax.dot_general(
            part, w[1, cut, :], (((0,), (0,)), ((), ())), preferred_element_type=F32)

    out_c[...] = acc[...].astype(BF16)

    for c in sends:
        c.wait_send()


def chain(key, places):
    n = key.shape[0]
    ids = jnp.arange(n)
    before = (key[:, None] < key[None, :]) | ((key[:, None] == key[None, :]) & (ids[:, None] < ids[None, :]))
    rank = jnp.sum(before.astype(jnp.int32), axis=0)
    here = (rank[None, :] == ids[:, None]).astype(jnp.int32)
    order = jnp.sum(here * ids[None, :], axis=1)
    same = (key[:, None] == key[None, :]) & (ids[:, None] < ids[None, :])
    joined = (jnp.sum(same.astype(jnp.int32), axis=0) > 0).astype(jnp.int32)
    cont = jnp.sum(here * joined[None, :], axis=1).astype(F32)
    spots = jnp.arange(places)
    last = jnp.sum((key[None, :] <= spots[:, None]).astype(jnp.int32), axis=1) - 1
    some = jnp.any(key[None, :] == spots[:, None], axis=1).astype(F32)
    return order, cont, jnp.maximum(last, 0), some


def shards(
    amp_tiles, amp_row, amp_col, amp_dest, amp_count,
    ladder_ints, ladder_present, cycle_ints, cycle_present,
):
    me = lax.axis_index("pair")
    y, z = me // NZ, me % NZ
    slots = jnp.arange(SLOTS)
    active = slots[None, :] < amp_count[:, None]
    owner = amp_dest // 2

    in_row = lax.dynamic_slice_in_dim(jnp.where(active, owner, -1), y * NZ, NZ, 0)
    goal = jnp.arange(NY) * NZ + z
    hit = (in_row[None] == goal[:, None, None]).astype(jnp.int32)
    rank = jnp.cumsum(hit, axis=2)
    first = [jnp.sum(jnp.where((hit > 0) & (rank == k + 1), slots, 0), axis=2) for k in range(2)]
    sel = jnp.stack(first, axis=2) + (jnp.arange(NZ) * SLOTS)[None, :, None]

    mine = (active & (owner == me)).astype(jnp.int32)
    rank_in = jnp.cumsum(mine, axis=1)
    place = amp_col * 2 + amp_dest % 2
    key = [
        jnp.sum(jnp.where((mine > 0) & (rank_in == k + 1), place - 48, 0), axis=1) + 48 for k in range(2)]
    order, cont, last, some = chain(jnp.stack(key, axis=1).reshape(-1), 48)

    def row(table):
        return lax.dynamic_index_in_dim(table, me, 0, keepdims=False)

    a_key = jnp.where(row(active), row(amp_row) * NCT + row(amp_col), 48)
    a_order, a_cont, a_last, a_some = chain(a_key, 48)

    smem = pl.BlockSpec(memory_space=pltpu.SMEM)
    vmem = pl.BlockSpec(memory_space=pltpu.VMEM)
    dma = pltpu.SemaphoreType.DMA
    out = jax.ShapeDtypeStruct((2 * TILE, COLS), BF16)
    return pl.pallas_call(
        kernel,
        out_shape=(out, out),
        in_specs=[smem] * 11 + [vmem, vmem, pl.BlockSpec(memory_space=pl.ANY)],
        out_specs=(vmem, vmem),
        scratch_shapes=[
            pltpu.VMEM((2, NCT * TILE, COLS), BF16),
            pltpu.VMEM((NZ * SLOTS, PART, TILE), BF16),
            pltpu.VMEM((96, PART, TILE), BF16),
            pltpu.VMEM((128, PART, TILE), BF16),
            pltpu.VMEM((128, PART, TILE), F32),
            pltpu.VMEM((NCT, TILE, 2 * TILE), BF16),
            pltpu.VMEM((SLOTS, TILE, TILE), BF16),
            pltpu.VMEM((SLOTS, TILE, TILE), F32),
            pltpu.VMEM((2 * TILE, NCT * TILE), BF16),
            pltpu.VMEM((2 * TILE, COLS), F32),
            dma((2,)),
            dma((2, HALF)), dma((2, HALF)), dma((2, HALF)), dma((2, HALF)),
            dma((2, NZ)), dma((2, NZ)), dma((2, NZ)), dma((2, NZ)),
            dma((3,)), dma((3,)), dma((4,)), dma((4,)), dma((5,)), dma((5,)),
        ],
        compiler_params=pltpu.CompilerParams(
            collective_id=0, has_side_effects=True, vmem_limit_bytes=40 * 2**20),
        cost_estimate=pl.CostEstimate(flops=1_300_000_000, bytes_accessed=3_000_000, transcendentals=0),
    )(
        ladder_present.reshape(-1), cycle_present.reshape(-1), sel.reshape(-1),
        order, cont, last, some, a_order, a_cont, a_last, a_some,
        ladder_ints, cycle_ints, amp_tiles,
    )


def solution(mesh):
    placed = (
        P("pair", None, None), P(), P(), P(), P(),
        P("pair", "ints"), P(None, "ints"), P("pair", "ints"), P(None, "ints"),
    )
    return jax.shard_map(
        shards,
        mesh=mesh,
        in_specs=placed,
        out_specs=(P("pair", "ints"), P("pair", "ints")),
        check_vma=False,
    )
```

time: 437 us -> 93.9 us (0.21)
  the two profiles are of different devices: /device:TPU:2 before, /device:TPU:1 now
where the time goes in v1:
time: 93.9 us; the launch traced here: 93.5 us
  Pallas kernels  83.2 us (89%)
  local copies, waits for them, and re-layouts  6.45 us (7%)
  other arithmetic  3.07 us (3%)
    pallas_call x1, Pallas kernels, shards(): pl.pallas_call(kernel, out_shape=(out, out), in_specs=[smem] * 11 + [vmem...  83.2 us
    unnamed x15, local copies, waits for them, and re-layouts  5.72 us

profile of v1, /device:TPU:1, one launch (start us, length us, event | category | flops | bytes accessed | tf_op | source)
XLA Modules:
  0.0 93.5 jit_solution(5078005049066903923)
XLA Ops:
  0.6 0.0 copy-start
  0.6 0.0 copy-start.1
  0.7 0.6 copy-done
  1.3 0.1 constant_dynamic-slice_fusion.1
  1.4 0.1 copy.44
  1.5 0.8 copy.33
  2.3 0.1 reshape.75.lp
  2.4 0.8 copy.34
  3.1 0.1 reshape.76.cp
  3.2 0.8 copy.40
  4.0 0.8 copy.35
  4.8 0.7 broadcast_compare_fusion.1
  5.6 0.1 convert_reduce_fusion.3
  5.7 0.1 fusion.7
  5.8 0.1 convert_reduce_fusion.4
  5.9 0.1 select_reduce_fusion.6
  6.0 0.2 reduce_window_sum.23
  6.2 0.2 select_reduce_fusion.3
  6.4 0.1 copy.41
  6.5 0.1 lt.115
  6.6 0.1 convert_reduce_fusion.2
  6.7 0.1 fusion.4
  6.9 0.1 convert_reduce_fusion
  7.0 0.1 select_reduce_fusion
  7.1 0.1 compare_convert_fusion
  7.2 0.7 reduce_window_sum.22
  7.9 0.3 select_reduce_fusion.5
  8.2 0.0 copy-start.3
  8.2 0.0 copy-start.2
  8.2 0.1 copy.39
  8.3 0.1 add.91.sel
  8.5 0.0 copy-done.1
  8.5 0.5 copy-done.3
  9.0 0.0 copy-done.2
  9.0 83.2 %shard_map.104 = (bf16[256,384]{1,0:T(8,128)(2,1)S(1)}, bf16[256,384]{1,0:T(8,128)(2,1)S(1)}) custom-call(s32[72]{0:T(128)S(1)} %reshape.75.lp, s32[72]{0:T(128)S(1)} %reshape.76.cp, s32[128]{0:T(128)S(1)} %add.91.sel, s32[128]{0:T(128)S(1)} %get-tuple-element.11.order, f32[128]{0:T(128)S(1)} %convert_element_type.57.cont, s32[48]{0:T(128)S(1)} %get-tuple-element.19.last, ...), custom_call_target="tpu_custom_call" | custom-call | flops 1300000000 | bytes 3000000 | tf_op jit(solution)/shard_map/pallas_call | solution.py:284
  92.2 0.7 copy.47
  92.9 0.7 copy.48
  (15 shorter events, 0.1 us)
Async XLA Ops:
  0.6 0.7 copy-start
  0.6 7.8 %copy-start.1 = (bf16[24,128,128]{2,1,0:T(8,128)(2,1)S(1)}, bf16[24,128,128]{2,1,0:T(8,128)(2,1)}, u32[]{:S(2)}) copy-start(bf16[24,128,128]{2,1,0:T(8,128)(2,1)} %tiles.1) | copy-start | bytes 2359300
  8.2 0.8 copy-start.3
  8.2 0.8 copy-start.2

commit v2 on v1

v2 whole, which is shorter than its diff:
```python
import jax
import jax.numpy as jnp
from jax import lax
from jax.experimental import pallas as pl
from jax.experimental.pallas import tpu as pltpu
from jax.sharding import PartitionSpec as P

TILE = 128
NCT = 24
SLOTS = 24
NY = 4
NZ = 16
NX = 4
PART = 16
ROWS = 48
COLS = 384
HALF = NZ // 2
DEPTH = NZ * ROWS
LAG = 2
PACE = (15,)
MESH = pl.DeviceIdType.MESH
F32 = jnp.float32
BF16 = jnp.bfloat16
I32 = jnp.int32


def iota(shape, dim):
    return lax.broadcasted_iota(I32, shape, dim)


def chain(down, across, value):
    i, j = iota((128, 128), 0), iota((128, 128), 1)
    tie = down == across
    rank = jnp.sum(jnp.where((across < down) | (tie & (j < i)), 1, 0), axis=1, keepdims=True)
    joined = jnp.max(jnp.where(tie & (j < i), 1, 0), axis=1, keepdims=True)
    here = rank == j
    order = jnp.sum(jnp.where(here, value, 0), axis=0, keepdims=True)
    cont = jnp.sum(jnp.where(here, joined, 0), axis=0, keepdims=True)
    last = jnp.sum(jnp.where(down <= j, 1, 0), axis=0, keepdims=True) - 1
    some = jnp.max(jnp.where(down == j, 1, 0), axis=0, keepdims=True)
    return order, cont, jnp.maximum(last, 0), some


def kernel(
    dest, col, row, count, lp, cp, wl, wr, tiles,
    out_l, out_c,
    w, t, zsend, zrecv, pre, bt, a_src, a_pre, a, acc_l, acc_c,
    dest_v, col_v, row_v, count_v, w_in, lp_s, cp_s, count_s, sel_v, tab_v, sel_s, tab_s,
    loc, zw_s, zw_r, y1_s, y1_r, y2_s, y2_r, ty_s, ty_r, tz_s, tz_r, xs_s, xs_r, co_s, co_r,
):
    p = lax.axis_index("pair")
    i = lax.axis_index("ints")
    y, z = p // NZ, p % NZ
    x, core = i // 2, i % 2

    def at(yy, zz):
        return (lax.rem(yy + NY, NY) * NZ + lax.rem(zz + NZ, NZ), i)

    def at_x(xx):
        return (p, lax.rem(xx + NX, NX) * 2 + core)

    zn = (at(y, z + 1), at(y, z - 1))
    yn = (at(y + 1, z), at(y - 1, z))
    xn = (at_x(x + 1), at_x(x - 1))
    twin = (p, x * 2 + 1 - core)

    pairs = [
        (tiles.at[:, pl.ds(pl.multiple_of(PART * i, PART), PART), :], t.at[pl.ds(y * SLOTS, SLOTS)]),
        (wl, w_in.at[0]), (wr, w_in.at[1]), (lp, lp_s), (cp, cp_s),
        (dest, dest_v), (count, count_s), (count, count_v), (col, col_v), (row, row_v), (tiles, a_src),
    ]
    local = [pltpu.make_async_copy(src, dst, loc.at[n]) for n, (src, dst) in enumerate(pairs)]
    for c in local:
        c.start()

    barrier = pltpu.get_barrier_semaphore()
    greet = [at(y, z + d) for d in range(1, NZ)] + [at(y + d, z) for d in range(1, NY)] + [*xn, twin]
    for dev in greet:
        pl.semaphore_signal(barrier, inc=1, device_id=dev, device_id_type=MESH)

    for c in local[1:5]:
        c.wait()
    for k, present in enumerate((lp_s, cp_s)):
        for g in range(ROWS // PART):
            line = (3 * p + g) // 8
            for n in range(COLS // TILE):
                keep = present[n, line].astype(F32)
                block = w_in[k, g * PART:(g + 1) * PART, n * TILE:(n + 1) * TILE].astype(F32)
                w[k, pl.ds(pl.multiple_of(ROWS * p + g * PART, PART), PART), n * TILE:(n + 1) * TILE] = (
                    block * keep).astype(BF16)

    for c in local[5:7]:
        c.wait()
    for ys in range(NY):
        source = ys * NZ + z
        slot = iota((SLOTS, TILE), 0)
        owner = jnp.sum(
            jnp.where(iota((SLOTS, 64), 1) == source, dest_v[...], 0), axis=1, keepdims=True)
        owner = lax.shift_right_logical(owner, 1)
        hit = (owner == y * NZ + iota((SLOTS, TILE), 1)) & (slot < count_s[0, source])
        first = jnp.min(jnp.where(hit, slot, 99), axis=0, keepdims=True)
        second = jnp.max(jnp.where(hit, slot, 0), axis=0, keepdims=True)
        sel_v[2 * ys:2 * ys + 1, :] = jnp.clip(first, 0, SLOTS - 1) + ys * SLOTS
        sel_v[2 * ys + 1:2 * ys + 2, :] = jnp.clip(second, 0, SLOTS - 1) + ys * SLOTS
    sel_copy = pltpu.make_async_copy(sel_v, sel_s, loc.at[11])
    sel_copy.start()
    local[0].wait()
    pl.semaphore_wait(barrier, len(greet))

    sends = []

    def send(src, dst, ss, rs, dev):
        c = pltpu.make_async_remote_copy(
            src_ref=src, dst_ref=dst, send_sem=ss, recv_sem=rs, device_id=dev, device_id_type=MESH)
        c.start()
        sends.append(c)

    def arrived(buf, ss, rs, dev):
        pltpu.make_async_remote_copy(
            src_ref=buf, dst_ref=buf, send_sem=ss, recv_sem=rs, device_id=dev, device_id_type=MESH).wait_recv()

    def w_at(yy, zz, part=None):
        q = lax.rem(yy + NY, NY) * NZ + lax.rem(zz + NZ, NZ)
        rows = pl.ds(pl.multiple_of(q * ROWS, PART), ROWS)
        if part is None:
            return w.at[:, rows, :]
        return w.at[part, rows, :]

    def t_at(yy):
        return t.at[pl.ds(lax.rem(yy + NY, NY) * SLOTS, SLOTS)]

    def group(g):
        if g == 0:
            return [(0, z)]
        if g == HALF:
            return [(NZ - 1, z - HALF)]
        return [(2 * g - 1, z - g), (2 * g, z + g)]

    def y_forward(g):
        for j, zz in group(g):
            for d in range(2):
                send(w_at(y, zz), w_at(y, zz), y1_s.at[d, j], y1_r.at[d, j], yn[d])

    def y_relay(g):
        for j, zz in group(g):
            for d in range(2):
                yy = y - 1 if d == 0 else y + 1
                arrived(w_at(yy, zz), y1_s.at[d, j], y1_r.at[d, j], yn[d])
                send(w_at(yy, zz, d), w_at(yy, zz, d), y2_s.at[d, j], y2_r.at[d, j], yn[d])

    def z_send(s, d):
        zz = z - s if d == 0 else z + s
        part = d if s == HALF - 1 else None
        send(w_at(y, zz, part), w_at(y, zz, part), zw_s.at[d, s], zw_r.at[d, s], zn[d])

    def z_wait(s, d):
        zz = z - s - 1 if d == 0 else z + s + 1
        part = d if s == HALF - 1 else None
        arrived(w_at(y, zz, part), zw_s.at[d, s], zw_r.at[d, s], zn[d])

    for dy in range(1, NY):
        send(t_at(y), t_at(y), ty_s.at[dy - 1], ty_r.at[dy - 1], at(y + dy, z))
    for d in range(2):
        z_send(0, d)
    y_forward(0)

    for dy in range(1, NY):
        arrived(t_at(y - dy), ty_s.at[dy - 1], ty_r.at[dy - 1], at(y + dy, z))
    sel_copy.wait()

    def choose(zz, _):
        for j in range(8):
            zsend[zz * 8 + j] = t[sel_s[j, zz]]
        return 0

    lax.fori_loop(0, NZ, choose, 0)
    for j in range(8):
        zrecv[z * 8 + j] = zsend[z * 8 + j]

    todo = sorted(range(1, NZ), key=lambda d: (-min(d, NZ - d), d))

    def t_sends(num):
        for d in todo[:num]:
            zz = lax.rem(z + d, NZ)
            send(zsend.at[pl.ds(zz * 8, 8)], zrecv.at[pl.ds(z * 8, 8)], tz_s.at[d - 1], tz_r.at[d - 1], at(y, zz))
        del todo[:num]

    def place_a(j, run):
        run = a_src[tab_s[4, j]].astype(F32) + tab_s[5, j].astype(F32) * run
        a_pre[j] = run
        return run

    def tables():
        for c in local[7:10]:
            c.wait()
        slot = iota((SLOTS, 64), 0)
        to = dest_v[...]
        mine = (slot < count_v[...]) & (lax.shift_right_logical(to, 1) == p)
        first = jnp.min(jnp.where(mine, slot, 99), axis=0, keepdims=True)
        second = jnp.max(jnp.where(mine, slot, -1), axis=0, keepdims=True)
        place = col_v[...] * 2 + (to & 1) - 48
        key0 = jnp.sum(jnp.where(mine & (slot == first), place, 0), axis=0, keepdims=True) + 48
        key1 = jnp.sum(
            jnp.where(mine & (slot == second) & (second > first), place, 0), axis=0, keepdims=True) + 48
        across = jnp.broadcast_to(jnp.concatenate([key0, key1], axis=1), (128, 128))
        n = iota((128, 128), 0)
        value = (n & 15) * 8 + (lax.shift_right_logical(n, 4) & 3) * 2 + lax.shift_right_logical(n, 6)
        rows = list(chain(across.T, across, value))
        own = jnp.sum(
            jnp.where(iota((SLOTS, 64), 1) == p, row_v[...] * NCT + col_v[...], 0),
            axis=1, keepdims=True)
        own = jnp.where(iota((SLOTS, 1), 0) < count_s[0, p], own, 48)
        own = jnp.concatenate([own, jnp.full((128 - SLOTS, 1), 99, I32)], axis=0)
        down = jnp.broadcast_to(own, (128, 128))
        rows += chain(down, down.T, n)
        for n, line in enumerate(rows):
            tab_v[n:n + 1, :] = jnp.clip(line, 0, 127 if n < 4 else SLOTS - 1)
        c = pltpu.make_async_copy(tab_v, tab_s, loc.at[12])
        c.start()
        return c

    for s in range(HALF):
        for d in range(2):
            z_wait(s, d)
            if s + 1 < HALF:
                z_send(s + 1, d)
        y_forward(s + 1)
        t_sends(PACE[min(s, len(PACE) - 1)])
        if s == 0:
            tab_copy = tables()
        if s == 1:
            tab_copy.wait()
            local[10].wait()
            lax.fori_loop(0, SLOTS, place_a, jnp.zeros((TILE, TILE), F32))
        if s in (2, 3):
            r = s - 2
            for c in range(NCT):
                q = r * NCT + c
                a[r * TILE:(r + 1) * TILE, c * TILE:(c + 1) * TILE] = (
                    a_pre[tab_s[6, q]] * tab_s[7, q].astype(F32)).astype(BF16)
        if s >= LAG:
            y_relay(s - LAG)

    for d in range(1, NZ):
        zz = lax.rem(z - d + NZ, NZ)
        arrived(zrecv.at[pl.ds(zz * 8, 8)], tz_s.at[d - 1], tz_r.at[d - 1], at(y, z + d))

    def add_up(j, run):
        run = zrecv[tab_s[0, j]].astype(F32) + tab_s[1, j].astype(F32) * run
        pre[j] = run
        return run

    lax.fori_loop(0, 128, add_up, jnp.zeros((PART, TILE), F32), unroll=8)

    def bt_at(ii, lo=0, num=NCT):
        return bt.at[pl.ds(lo, num), pl.ds(pl.multiple_of(ii * PART, PART), PART), :]

    for q in range(2 * NCT):
        c, r = q // 2, q % 2
        bt[c, pl.ds(pl.multiple_of(i * PART, PART), PART), r * TILE:(r + 1) * TILE] = (
            pre[tab_s[2, q]] * tab_s[3, q].astype(F32)).astype(BF16)

    for d in range(2):
        send(bt_at(i), bt_at(i), xs_s.at[d], xs_r.at[d], xn[d])
    send(bt_at(i), bt_at(i), co_s.at[0], co_r.at[0], twin)

    for g in range(HALF - LAG, HALF):
        y_relay(g)

    half = NCT // 2
    for d in range(2):
        ii = xn[1 - d][1]
        arrived(bt_at(ii), xs_s.at[d], xs_r.at[d], xn[d])
        send(bt_at(ii, d * half, half), bt_at(ii, d * half, half), xs_s.at[2 + d], xs_r.at[2 + d], xn[d])
        send(bt_at(ii), bt_at(ii), co_s.at[1 + d], co_r.at[1 + d], twin)
    y_relay(HALF)

    def ladder(yy, fresh=False):
        yy = lax.rem(yy + NY, NY)
        cut = pl.ds(pl.multiple_of(yy * DEPTH, DEPTH), DEPTH)
        add = jnp.dot(a[:, cut], w[0, cut, :], preferred_element_type=F32)
        acc_l[...] = add if fresh else acc_l[...] + add

    def cycle(yy, fresh=False):
        yy = lax.rem(yy + NY, NY)
        cut = pl.ds(pl.multiple_of(yy * DEPTH, DEPTH), DEPTH)
        part = bt[pl.ds(yy * (DEPTH // TILE), DEPTH // TILE)].reshape(DEPTH, 2 * TILE)
        add = lax.dot_general(part, w[1, cut, :], (((0,), (0,)), ((), ())), preferred_element_type=F32)
        acc_c[...] = add if fresh else acc_c[...] + add

    ladder(y, True)
    far = at_x(x + 2)[1]
    for d in range(2):
        arrived(bt_at(far, d * half, half), xs_s.at[2 + d], xs_r.at[2 + d], xn[d])
        send(bt_at(far, d * half, half), bt_at(far, d * half, half), co_s.at[3 + d], co_r.at[3 + d], twin)
    ladder(y + 1)
    ladder(y - 1)

    def other(ii):
        return lax.div(ii, 2) * 2 + 1 - lax.rem(ii, 2)

    arrived(bt_at(other(i)), co_s.at[0], co_r.at[0], twin)
    for d in range(2):
        arrived(bt_at(other(xn[1 - d][1])), co_s.at[1 + d], co_r.at[1 + d], twin)
    for d in range(2):
        arrived(bt_at(other(far), d * half, half), co_s.at[3 + d], co_r.at[3 + d], twin)
    cycle(y, True)
    cycle(y + 1)
    cycle(y - 1)
    for g in range(HALF + 1):
        for j, zz in group(g):
            for d in range(2):
                arrived(w_at(y + 2, zz, d), y2_s.at[d, j], y2_r.at[d, j], yn[d])
    ladder(y + 2)
    out_l[...] = acc_l[...].astype(BF16)
    cycle(y + 2)
    out_c[...] = acc_c[...].astype(BF16)

    for c in sends:
        c.wait_send()


def shards(
    amp_tiles, amp_row, amp_col, amp_dest, amp_count,
    ladder_ints, ladder_present, cycle_ints, cycle_present,
):
    vmem = pl.BlockSpec(memory_space=pltpu.VMEM)
    dma = pltpu.SemaphoreType.DMA
    out = jax.ShapeDtypeStruct((2 * TILE, COLS), BF16)
    return pl.pallas_call(
        kernel,
        out_shape=(out, out),
        in_specs=[pl.BlockSpec(memory_space=pl.ANY)] * 9,
        out_specs=(vmem, vmem),
        scratch_shapes=[
            pltpu.VMEM((2, NCT * TILE, COLS), BF16),
            pltpu.VMEM((NY * SLOTS, PART, TILE), BF16),
            pltpu.VMEM((128, PART, TILE), BF16),
            pltpu.VMEM((128, PART, TILE), BF16),
            pltpu.VMEM((128, PART, TILE), F32),
            pltpu.VMEM((NCT, TILE, 2 * TILE), BF16),
            pltpu.VMEM((SLOTS, TILE, TILE), BF16),
            pltpu.VMEM((SLOTS, TILE, TILE), F32),
            pltpu.VMEM((2 * TILE, NCT * TILE), BF16),
            pltpu.VMEM((2 * TILE, COLS), F32),
            pltpu.VMEM((2 * TILE, COLS), F32),
            pltpu.VMEM((SLOTS, 64), I32), pltpu.VMEM((SLOTS, 64), I32), pltpu.VMEM((SLOTS, 64), I32),
            pltpu.VMEM((1, 64), I32), pltpu.VMEM((2, ROWS, COLS), BF16),
            pltpu.SMEM((3, NCT), I32), pltpu.SMEM((3, NCT), I32), pltpu.SMEM((1, 64), I32),
            pltpu.VMEM((8, TILE), I32), pltpu.VMEM((8, TILE), I32),
            pltpu.SMEM((8, TILE), I32), pltpu.SMEM((8, TILE), I32),
            dma((13,)),
            dma((2, HALF)), dma((2, HALF)),
            dma((2, NZ)), dma((2, NZ)), dma((2, NZ)), dma((2, NZ)),
            dma((NY - 1,)), dma((NY - 1,)), dma((NZ - 1,)), dma((NZ - 1,)),
            dma((4,)), dma((4,)), dma((5,)), dma((5,)),
        ],
        compiler_params=pltpu.CompilerParams(
            collective_id=0, has_side_effects=True, vmem_limit_bytes=56 * 2**20),
        cost_estimate=pl.CostEstimate(flops=1_300_000_000, bytes_accessed=3_000_000, transcendentals=0),
    )(
        amp_dest.T, amp_col.T, amp_row.T, amp_count.reshape(1, -1), ladder_present.T, cycle_present.T,
        ladder_ints, cycle_ints, amp_tiles,
    )


def solution(mesh):
    placed = (
        P("pair", None, None), P(), P(), P(), P(),
        P("pair", "ints"), P(None, "ints"), P("pair", "ints"), P(None, "ints"),
    )
    return jax.shard_map(
        shards,
        mesh=mesh,
        in_specs=placed,
        out_specs=(P("pair", "ints"), P("pair", "ints")),
        check_vma=False,
    )
```

time: 93.9 us -> 88.3 us (0.940)
  local copies, waits for them, and re-layouts: 6.45 us -> 2.34 us
  other arithmetic: 3.07 us -> 0 us
  Pallas kernels: 83.2 us -> 85.1 us
    unnamed x15 -> x4, local copies, waits for them, and re-layouts: 5.72 us -> 2.34 us
    pallas_call x1, Pallas kernels: 83.2 us -> 85.1 us  [shards(): pl.pallas_call(kernel, out_shape=(out, out), in_specs=[pl.BlockSpec(memor...]
    reduce_sum x8 -> x0, other arithmetic: 1.07 us -> none  [the longest x1 0.3 us: shards(): jnp.sum(jnp.where((hit > 0) & (rank == k + 1), slots, 0), axis=2)]
where the time goes in v2:
time: 88.3 us; the launch traced here: 88.1 us
  Pallas kernels  85.1 us (96%)
  local copies, waits for them, and re-layouts  2.34 us (3%)
    pallas_call x1, Pallas kernels, shards(): pl.pallas_call(kernel, out_shape=(out, out), in_specs=[pl.BlockSpec(memor...  85.1 us
    unnamed x4, local copies, waits for them, and re-layouts  2.34 us

profile of v2, /device:TPU:1, one launch (start us, length us, event | category | flops | bytes accessed | tf_op | source)
XLA Modules:
  0.0 88.1 jit_solution(17964301367174347344)
XLA Ops:
  0.6 85.1 %shard_map.104 = (bf16[256,384]{1,0:T(8,128)(2,1)}, bf16[256,384]{1,0:T(8,128)(2,1)}) custom-call(s32[24,64]{1,0:T(8,128)} %bitcast.6, s32[24,64]{1,0:T(8,128)} %bitcast.7, s32[24,64]{1,0:T(8,128)} %bitcast.8, s32[1,64]{1,0:T(1,128)} %bitcast.11, s32[3,24]{1,0:T(4,128)} %bitcast.9, s32[3,24]{1,0:T(4,128)} %bitcast.10, bf16[48,384]{1,0:T(8,128)(2,1)} %wl.1, ...), custom_call_target="tpu_custom_call" | custom-call | flops 1300000000 | bytes 3000000 | tf_op jit(solution)/shard_map/pallas_call | solution.py:330
  85.8 0.0 copy-start
  85.8 1.7 %copy.13 = bf16[256,384]{1,0:T(8,128)(2,1)} copy(bf16[256,384]{1,0:T(8,128)(2,1)} %get-tuple-element.4) | data formatting | bytes 393216
  87.4 0.0 copy-done
  87.4 0.7 copy.14
Async XLA Ops:
  85.8 1.7 %copy-start = (bf16[256,384]{1,0:T(8,128)(2,1)S(1)}, bf16[256,384]{1,0:T(8,128)(2,1)}, u32[]{:S(2)}) copy-start(bf16[256,384]{1,0:T(8,128)(2,1)} %get-tuple-element.5) | copy-start | bytes 589828

commit v3 on v2

v3 whole, which is shorter than its diff:
```python
import jax
import jax.numpy as jnp
from jax import lax
from jax.experimental import pallas as pl
from jax.experimental.pallas import tpu as pltpu
from jax.sharding import PartitionSpec as P

TILE = 128
NCT = 24
SLOTS = 24
NY = 4
NZ = 16
NX = 4
PART = 16
ROWS = 48
COLS = 384
DEPTH = NZ * ROWS
LAG = 4
W_REACH = (8, 7)
T_REACH = (7, 8)
CUTS = 2
RIM_OUT = (2, 4, 6, 9, 11, 13)
ROOM = 56
MESH = pl.DeviceIdType.MESH
F32 = jnp.float32
BF16 = jnp.bfloat16
I32 = jnp.int32


def iota(shape, dim):
    return lax.broadcasted_iota(I32, shape, dim)


def chain(down, across, value):
    i, j = iota((128, 128), 0), iota((128, 128), 1)
    tie = down == across
    rank = jnp.sum(jnp.where((across < down) | (tie & (j < i)), 1, 0), axis=1, keepdims=True)
    joined = jnp.max(jnp.where(tie & (j < i), 1, 0), axis=1, keepdims=True)
    here = rank == j
    order = jnp.sum(jnp.where(here, value, 0), axis=0, keepdims=True)
    cont = jnp.sum(jnp.where(here, joined, 0), axis=0, keepdims=True)
    last = jnp.sum(jnp.where(down <= j, 1, 0), axis=0, keepdims=True) - 1
    some = jnp.max(jnp.where(down == j, 1, 0), axis=0, keepdims=True)
    return order, cont, jnp.maximum(last, 0), some


def kernel(
    dest, col, row, count, lp, cp, wl, wr, tiles,
    out_l, out_c,
    w, ysend, yrecv, pre, bt, a_src, a_pre, a, acc_l, acc_c, acc_p, from_mate, ams, ams_pre, am,
    dest_v, col_v, row_v, count_v, w_in, lp_s, cp_s, count_s, sel_v, tab_v, sel_s, tab_s,
    loc, zw_s, zw_r, y1_s, y1_r, y2_s, y2_r, ty_s, ty_r, tz_s, tz_r, xs_s, xs_r, co_s, co_r,
    ax_s, ax_r, ac_s, ac_r, ay_s, ay_r, pc_s, pc_r, *t,
):
    p = lax.axis_index("pair")
    i = lax.axis_index("ints")
    y, z = p // NZ, p % NZ
    x, core = i // 2, i % 2

    def at(yy, zz):
        return (lax.rem(yy + NY, NY) * NZ + lax.rem(zz + NZ, NZ), i)

    def at_x(xx):
        return (p, lax.rem(xx + NX, NX) * 2 + core)

    zn = (at(y, z + 1), at(y, z - 1))
    odd = lax.rem(y, 2)
    ym, yr, yf = y + 1 - 2 * odd, lax.rem(y + 3 + 2 * odd, NY), lax.rem(y + 2, NY)
    yn = (at(ym, z), at(yr, z))
    xn = (at_x(x + 1), at_x(x - 1))
    twin = (p, x * 2 + 1 - core)

    pairs = [
        (tiles.at[:, pl.ds(pl.multiple_of(PART * i, PART), PART), :], t[0]),
        (wl, w_in.at[0]), (wr, w_in.at[1]), (lp, lp_s), (cp, cp_s),
        (dest, dest_v), (count, count_s), (count, count_v), (col, col_v), (row, row_v), (tiles, a_src),
    ]
    local = [pltpu.make_async_copy(src, dst, loc.at[n]) for n, (src, dst) in enumerate(pairs)]
    for c in local:
        c.start()

    barrier = pltpu.get_barrier_semaphore()
    greet = [*zn, *xn, twin] + [at(y + d, z) for d in range(1, NY)]
    for dev in greet:
        pl.semaphore_signal(barrier, inc=1, device_id=dev, device_id_type=MESH)

    sends = []

    def send(src, dst, ss, rs, dev):
        c = pltpu.make_async_remote_copy(
            src_ref=src, dst_ref=dst, send_sem=ss, recv_sem=rs, device_id=dev, device_id_type=MESH)
        c.start()
        sends.append(c)

    def arrived(buf, ss, rs, dev):
        pltpu.make_async_remote_copy(
            src_ref=buf, dst_ref=buf, send_sem=ss, recv_sem=rs, device_id=dev, device_id_type=MESH).wait_recv()

    def w_at(yy, zz, part=None):
        q = lax.rem(yy + NY, NY) * NZ + lax.rem(zz + NZ, NZ)
        rows = pl.ds(pl.multiple_of(q * ROWS, PART), ROWS)
        if part is None:
            return w.at[:, rows, :]
        return w.at[part, rows, :]

    def t_send(s, d, h):
        if s < T_REACH[d]:
            cut = pl.ds(h * (SLOTS // CUTS), SLOTS // CUTS)
            here, there = ((NZ - s) % NZ, NZ - s - 1) if d == 0 else (s, s + 1)
            src = t[here].at[cut]
            if s == 0:
                src = tiles.at[cut, pl.ds(pl.multiple_of(PART * i, PART), PART), :]
            send(src, t[there].at[cut], tz_s.at[d, s * CUTS + h], tz_r.at[d, s * CUTS + h], zn[d])

    def t_wait(s, d, h):
        if s < T_REACH[d]:
            cut = pl.ds(h * (SLOTS // CUTS), SLOTS // CUTS)
            arrived(t[NZ - s - 1 if d == 0 else s + 1].at[cut], tz_s.at[d, s * CUTS + h], tz_r.at[d, s * CUTS + h], zn[d])

    pl.semaphore_wait(barrier, len(greet))
    for h in range(CUTS):
        for d in range(2):
            t_send(0, d, h)

    for c in local[1:5]:
        c.wait()
    for k, present in enumerate((lp_s, cp_s)):
        for g in range(ROWS // PART):
            line = (3 * p + g) // 8
            for n in range(COLS // TILE):
                keep = present[n, line].astype(F32)
                block = w_in[k, g * PART:(g + 1) * PART, n * TILE:(n + 1) * TILE].astype(F32)
                w[k, pl.ds(pl.multiple_of(ROWS * p + g * PART, PART), PART), n * TILE:(n + 1) * TILE] = (
                    block * keep).astype(BF16)

    reach = W_REACH
    steps = NZ // 2

    def group(g):
        if g == 0:
            return [(0, z)]
        near = [(NZ - g, z - g)] if g <= reach[0] else []
        return near + ([(g, z + g)] if g <= reach[1] else [])

    def y_forward(g):
        for j, zz in group(g):
            send(w_at(y, zz), w_at(y, zz), y1_s.at[1, j], y1_r.at[1, j], yn[1])
            send(w_at(y, zz, 1), w_at(y, zz, 1), y1_s.at[0, j], y1_r.at[0, j], yn[0])

    def y_relay(g):
        for j, zz in group(g):
            arrived(w_at(yr, zz), y1_s.at[1, j], y1_r.at[1, j], yn[1])
            arrived(w_at(ym, zz, 1), y1_s.at[0, j], y1_r.at[0, j], yn[0])
            e = int(j in RIM_OUT)
            part = w_at(ym if e else yr, zz, 1)
            send(part, part, y2_s.at[j], y2_r.at[j], yn[e])

    def z_send(s, d, k):
        zz = z - s if d == 0 else z + s
        if s < reach[d]:
            send(w_at(y, zz, k), w_at(y, zz, k), zw_s.at[d, 2 * s + k], zw_r.at[d, 2 * s + k], zn[d])

    def z_wait(s, d, k):
        zz = z - s - 1 if d == 0 else z + s + 1
        if s < reach[d]:
            arrived(w_at(y, zz, k), zw_s.at[d, 2 * s + k], zw_r.at[d, 2 * s + k], zn[d])

    for k in range(2):
        for d in range(2):
            z_send(0, d, k)
    y_forward(0)

    for c in local[5:8:2]:
        c.wait()
    slot = iota((SLOTS, 64), 0)
    used = slot < count_v[...]
    owner = lax.shift_right_logical(dest_v[...], 1)
    for yy in range(NY):
        hit = used & (owner == yy * NZ + z)
        first = jnp.min(jnp.where(hit, slot, SLOTS - 1), axis=0, keepdims=True)
        second = jnp.max(jnp.where(hit, slot, 0), axis=0, keepdims=True)
        sel_v[2 * yy:2 * yy + 1, :] = jnp.clip(first, 0, SLOTS - 1)
        sel_v[2 * yy + 1:2 * yy + 2, :] = jnp.clip(second, 0, SLOTS - 1)
    sel_copy = pltpu.make_async_copy(sel_v, sel_s, loc.at[11])
    sel_copy.start()
    local[0].wait()
    sel_copy.wait()

    def span(g):
        return (0, 1) if g == 0 else (NZ - 1, 1) if g == NZ // 2 else (2 * g - 1, 2)

    def y_piece(buf, dy, g):
        lo, num = span(g)
        return buf.at[pl.ds((dy * NZ + lo) * 2, num * 2)]

    def choose(g):
        far = [g] if g in (0, NZ // 2) else [NZ - g, g]
        for n, zz in enumerate([z + o for o in far]):
            zz = lax.rem(zz + NZ, NZ)
            for dy in (1, 2, 3, 0):
                yy = lax.rem(y + dy, NY)
                for j in range(2):
                    buf, row = (ysend, dy - 1) if dy else (yrecv, 0)
                    buf[(row * NZ + span(g)[0] + n) * 2 + j] = t[far[n]][sel_s[2 * yy + j, y * NZ + zz]]
        for dy in (1, 3, 2):
            send(y_piece(ysend, dy - 1, g), y_piece(yrecv, dy, g),
                 ty_s.at[dy - 1, g], ty_r.at[dy - 1, g], at(y + dy, z))

    choose(0)

    def place_a(j, run):
        run = a_src[tab_s[4, j]].astype(F32) + tab_s[5, j].astype(F32) * run
        a_pre[j] = run
        return run

    def place_slices(j, run):
        run = t[0][tab_s[4, j]].astype(F32) + tab_s[5, j].astype(F32) * run
        ams_pre[j] = run
        return run

    def a_place(buf, r, c, first, second):
        q = r * NCT + (first * 6 + c if c < 6 else second * 6 + c - 6)
        return (buf[tab_s[6, q]] * tab_s[7, q].astype(F32)).astype(BF16)

    def part_rows(ii):
        return pl.ds(pl.multiple_of(ii * PART, PART), PART)

    def other(ii):
        return lax.div(ii, 2) * 2 + 1 - lax.rem(ii, 2)

    def spread(piece, xs, xr, cs, cr):
        def start():
            for n in range(2):
                for d in range(2):
                    send(piece(i, (d + n) % 2), piece(i, (d + n) % 2), xs.at[d, n], xr.at[d, n], xn[d])
            for h in range(2):
                send(piece(i, h), piece(i, h), cs.at[h], cr.at[h], twin)

        def near():
            for n in range(2):
                for d in range(2):
                    part = piece(xn[1 - d][1], (d + n) % 2)
                    arrived(part, xs.at[d, n], xr.at[d, n], xn[d])
                    if n == 0:
                        send(part, part, xs.at[d, 2], xr.at[d, 2], xn[d])
                    send(part, part, cs.at[2 + 2 * n + d], cr.at[2 + 2 * n + d], twin)

        def last():
            for d in range(2):
                part = piece(at_x(x + 2)[1], d)
                arrived(part, xs.at[d, 2], xr.at[d, 2], xn[d])
                send(part, part, cs.at[6 + d], cr.at[6 + d], twin)

        def finish():
            for h in range(2):
                arrived(piece(other(i), h), cs.at[h], cr.at[h], twin)
            for n in range(2):
                for d in range(2):
                    part = piece(other(xn[1 - d][1]), (d + n) % 2)
                    arrived(part, cs.at[2 + 2 * n + d], cr.at[2 + 2 * n + d], twin)
            for d in range(2):
                arrived(piece(other(at_x(x + 2)[1]), d), cs.at[6 + d], cr.at[6 + d], twin)

        return start, near, last, finish

    am_spread = spread(lambda ii, h: am.at[h, part_rows(ii), :], ax_s, ax_r, ac_s, ac_r)
    half = NCT // 2
    bt_spread = spread(lambda ii, h: bt.at[pl.ds(h * half, half), part_rows(ii), :], xs_s, xs_r, co_s, co_r)

    def tables():
        for c in (local[6], *local[8:10]):
            c.wait()
        to = dest_v[...]
        mine = used & (owner == p)
        first = jnp.min(jnp.where(mine, slot, 99), axis=0, keepdims=True)
        second = jnp.max(jnp.where(mine, slot, -1), axis=0, keepdims=True)
        place = col_v[...] * 2 + (to & 1) - 48
        key0 = jnp.sum(jnp.where(mine & (slot == first), place, 0), axis=0, keepdims=True) + 48
        key1 = jnp.sum(
            jnp.where(mine & (slot == second) & (second > first), place, 0), axis=0, keepdims=True) + 48
        across = jnp.broadcast_to(jnp.concatenate([key0, key1], axis=1), (128, 128))
        n = iota((128, 128), 0)
        dy = (y + NY - lax.shift_right_logical(n, 4)) & 3
        off = (n + NZ - z) & 15
        turn = jnp.where(off < 8, 2 * off, jnp.where(off == 8, NZ - 1, 31 - 2 * off))
        value = dy * 32 + turn * 2 + lax.shift_right_logical(n, 6)
        rows = list(chain(across.T, across, value))
        own = jnp.sum(
            jnp.where(iota((SLOTS, 64), 1) == p, row_v[...] * NCT + col_v[...], 0),
            axis=1, keepdims=True)
        own = jnp.where(iota((SLOTS, 1), 0) < count_s[0, p], own, 48)
        own = jnp.concatenate([own, jnp.full((128 - SLOTS, 1), 99, I32)], axis=0)
        down = jnp.broadcast_to(own, (128, 128))
        rows += chain(down, down.T, n)
        for n, line in enumerate(rows):
            tab_v[n:n + 1, :] = jnp.clip(line, 0, 127 if n < 4 else SLOTS - 1)
        c = pltpu.make_async_copy(tab_v, tab_s, loc.at[12])
        c.start()
        return c

    for s in range(steps):
        for k in range(2):
            for d in range(2):
                t_wait(s, d, k)
                t_send(s + 1, d, k)
            for d in range(2):
                z_wait(s, d, k)
                z_send(s + 1, d, k)
        choose(s + 1)
        y_forward(s + 1)
        if s == 0:
            tab_copy = tables()
        if s == 1:
            tab_copy.wait()
            lax.fori_loop(0, SLOTS, place_slices, jnp.zeros((PART, TILE), F32))
            for r in range(2):
                for c in range(12):
                    ams[r, :, c * TILE:(c + 1) * TILE] = a_place(ams_pre, r, c, ym, yf)
            send(ams, am.at[:, part_rows(i), :], ay_s.at[0], ay_r.at[0], yn[0])
        if s == 2:
            local[10].wait()
            lax.fori_loop(0, SLOTS, place_a, jnp.zeros((TILE, TILE), F32))
        if s == 3:
            arrived(am.at[:, part_rows(i), :], ay_s.at[0], ay_r.at[0], yn[0])
            am_spread[0]()
            for r in range(2):
                for c in range(12):
                    a[r * TILE:(r + 1) * TILE, c * TILE:(c + 1) * TILE] = a_place(a_pre, r, c, y, yr)
        if s == 5:
            am_spread[1]()
        if s == 7:
            am_spread[2]()
        if s >= LAG:
            y_relay(s - LAG)

    for g in range(steps + 1):
        for dy in (1, 3, 2):
            arrived(y_piece(yrecv, dy, g), ty_s.at[dy - 1, g], ty_r.at[dy - 1, g], at(y + dy, z))

    def add_up(j, run):
        run = yrecv[tab_s[0, j]].astype(F32) + tab_s[1, j].astype(F32) * run
        pre[j] = run
        return run

    lax.fori_loop(0, 128, add_up, jnp.zeros((PART, TILE), F32), unroll=8)

    for q in range(2 * NCT):
        c, r = q // 2, q % 2
        bt[c, part_rows(i), r * TILE:(r + 1) * TILE] = (pre[tab_s[2, q]] * tab_s[3, q].astype(F32)).astype(BF16)

    bt_spread[0]()
    for g in range(steps - LAG, steps + 1):
        y_relay(g)

    am_spread[3]()

    def wl_rows(yy):
        return w[0, pl.ds(pl.multiple_of(yy * DEPTH, DEPTH), DEPTH), :]

    def half_ladder(buf, acc):
        for n, yy in enumerate((y, yr)):
            left = buf[..., n * DEPTH:(n + 1) * DEPTH].reshape(2 * TILE, DEPTH)
            add = jnp.dot(left, wl_rows(yy), preferred_element_type=F32)
            acc[...] = acc[...] + add if n else add

    half_ladder(am, acc_p)
    send(acc_p, from_mate, pc_s.at[0], pc_r.at[0], yn[0])
    bt_spread[1]()
    half_ladder(a, acc_l)
    bt_spread[2]()

    def cycle(yy, fresh=False):
        cut = pl.ds(pl.multiple_of(yy * DEPTH, DEPTH), DEPTH)
        part = bt[pl.ds(yy * (DEPTH // TILE), DEPTH // TILE)].reshape(DEPTH, 2 * TILE)
        add = lax.dot_general(part, w[1, cut, :], (((0,), (0,)), ((), ())), preferred_element_type=F32)
        acc_c[...] = add if fresh else acc_c[...] + add

    bt_spread[3]()
    cycle(y, True)
    cycle(ym)
    cycle(yr)
    for g in range(steps + 1):
        for j, zz in group(g):
            arrived(w_at(yf, zz, 1), y2_s.at[j], y2_r.at[j], yn[int(j in RIM_OUT)])
    cycle(yf)
    out_c[...] = acc_c[...].astype(BF16)
    arrived(from_mate, pc_s.at[0], pc_r.at[0], yn[0])
    out_l[...] = (acc_l[...] + from_mate[...]).astype(BF16)

    for c in sends:
        c.wait_send()


def shards(
    amp_tiles, amp_row, amp_col, amp_dest, amp_count,
    ladder_ints, ladder_present, cycle_ints, cycle_present,
):
    vmem, anywhere = pl.BlockSpec(memory_space=pltpu.VMEM), pl.BlockSpec(memory_space=pl.ANY)
    dma = pltpu.SemaphoreType.DMA
    out = jax.ShapeDtypeStruct((2 * TILE, COLS), BF16)
    return pl.pallas_call(
        kernel,
        out_shape=(out, out),
        in_specs=[anywhere] * 9,
        out_specs=(vmem, vmem),
        scratch_shapes=[
            pltpu.VMEM((2, NCT * TILE, COLS), BF16),
            pltpu.VMEM((96, PART, TILE), BF16),
            pltpu.VMEM((128, PART, TILE), BF16),
            pltpu.VMEM((128, PART, TILE), F32),
            pltpu.VMEM((NCT, TILE, 2 * TILE), BF16),
            pltpu.VMEM((SLOTS, TILE, TILE), BF16),
            pltpu.VMEM((SLOTS, TILE, TILE), F32),
            pltpu.VMEM((2 * TILE, 2 * DEPTH), BF16),
            *[pltpu.VMEM((2 * TILE, COLS), F32)] * 4,
            pltpu.VMEM((2, PART, 2 * DEPTH), BF16),
            pltpu.VMEM((SLOTS, PART, TILE), F32),
            pltpu.VMEM((2, TILE, 2 * DEPTH), BF16),
            pltpu.VMEM((SLOTS, 64), I32), pltpu.VMEM((SLOTS, 64), I32), pltpu.VMEM((SLOTS, 64), I32),
            pltpu.VMEM((1, 64), I32), pltpu.VMEM((2, ROWS, COLS), BF16),
            pltpu.SMEM((3, NCT), I32), pltpu.SMEM((3, NCT), I32), pltpu.SMEM((1, 64), I32),
            pltpu.VMEM((8, 64), I32), pltpu.VMEM((8, TILE), I32),
            pltpu.SMEM((8, 64), I32), pltpu.SMEM((8, TILE), I32),
            dma((13,)),
            dma((2, 2 * NZ)), dma((2, 2 * NZ)),
            dma((2, NZ)), dma((2, NZ)), dma((NZ,)), dma((NZ,)),
            dma((NY - 1, 9)), dma((NY - 1, 9)), dma((2, 8 * CUTS)), dma((2, 8 * CUTS)),
            dma((2, 3)), dma((2, 3)), dma((8,)), dma((8,)), dma((2, 3)), dma((2, 3)), dma((8,)), dma((8,)),
            dma((1,)), dma((1,)), dma((1,)), dma((1,)),
            *[pltpu.VMEM((SLOTS, PART, TILE), BF16)] * NZ,
        ],
        compiler_params=pltpu.CompilerParams(
            collective_id=0, has_side_effects=True, vmem_limit_bytes=ROOM * 2**20),
        cost_estimate=pl.CostEstimate(flops=1_300_000_000, bytes_accessed=3_000_000, transcendentals=0),
    )(
        amp_dest.T, amp_col.T, amp_row.T, amp_count.reshape(1, -1), ladder_present.T, cycle_present.T,
        ladder_ints, cycle_ints, amp_tiles,
    )


def solution(mesh):
    placed = (
        P("pair", None, None), P(), P(), P(), P(),
        P("pair", "ints"), P(None, "ints"), P("pair", "ints"), P(None, "ints"),
    )
    return jax.shard_map(
        shards,
        mesh=mesh,
        in_specs=placed,
        out_specs=(P("pair", "ints"), P("pair", "ints")),
        check_vma=False,
    )
```

time: 88.3 us -> 70.6 us (0.80)
  Pallas kernels: 85.1 us -> 67.5 us
    pallas_call x1, Pallas kernels: 85.1 us -> 67.5 us  [shards(): pl.pallas_call(kernel, out_shape=(out, out), in_specs=[anywhere] * 9, out...]
where the time goes in v3:
time: 70.6 us; the launch traced here: 70.5 us
  Pallas kernels  67.5 us (96%)
  local copies, waits for them, and re-layouts  2.34 us (3%)
    pallas_call x1, Pallas kernels, shards(): pl.pallas_call(kernel, out_shape=(out, out), in_specs=[anywhere] * 9, out...  67.5 us
    unnamed x4, local copies, waits for them, and re-layouts  2.34 us

profile of v3, /device:TPU:1, one launch (start us, length us, event | category | flops | bytes accessed | tf_op | source)
XLA Modules:
  0.0 70.5 jit_solution(2589419474341358139)
XLA Ops:
  0.6 67.5 %shard_map.104 = (bf16[256,384]{1,0:T(8,128)(2,1)}, bf16[256,384]{1,0:T(8,128)(2,1)}) custom-call(s32[24,64]{1,0:T(8,128)} %bitcast.6, s32[24,64]{1,0:T(8,128)} %bitcast.7, s32[24,64]{1,0:T(8,128)} %bitcast.8, s32[1,64]{1,0:T(1,128)} %bitcast.11, s32[3,24]{1,0:T(4,128)} %bitcast.9, s32[3,24]{1,0:T(4,128)} %bitcast.10, bf16[48,384]{1,0:T(8,128)(2,1)} %wl.1, ...), custom_call_target="tpu_custom_call" | custom-call | flops 1300000000 | bytes 3000000 | tf_op jit(solution)/shard_map/pallas_call | solution.py:401
  68.1 0.0 copy-start
  68.1 1.7 %copy.13 = bf16[256,384]{1,0:T(8,128)(2,1)} copy(bf16[256,384]{1,0:T(8,128)(2,1)} %get-tuple-element.4) | data formatting | bytes 393216
  69.8 0.0 copy-done
  69.8 0.7 copy.14
Async XLA Ops:
  68.1 1.7 %copy-start = (bf16[256,384]{1,0:T(8,128)(2,1)S(1)}, bf16[256,384]{1,0:T(8,128)(2,1)}, u32[]{:S(2)}) copy-start(bf16[256,384]{1,0:T(8,128)(2,1)} %get-tuple-element.5) | copy-start | bytes 589828

commit v4 on v3

--- a/solution.py
+++ b/solution.py
@@ -18,8 +18,10 @@
 LAG = 4
 W_REACH = (8, 7)
 T_REACH = (7, 8)
+LAST = (NZ - T_REACH[0], T_REACH[1])
 CUTS = 2
-RIM_OUT = (2, 4, 6, 9, 11, 13)
+BEHIND = 0
+RIM_OUT = (3, 5, 6, 7, 8, 9, 11, 13)
 ROOM = 56
 MESH = pl.DeviceIdType.MESH
 F32 = jnp.float32
@@ -48,7 +50,7 @@
     dest, col, row, count, lp, cp, wl, wr, tiles,
     out_l, out_c,
     w, ysend, yrecv, pre, bt, a_src, a_pre, a, acc_l, acc_c, acc_p, from_mate, ams, ams_pre, am,
-    dest_v, col_v, row_v, count_v, w_in, lp_s, cp_s, count_s, sel_v, tab_v, sel_s, tab_s,
+    dest_v, col_v, row_v, count_v, w_in, lp_s, cp_s, count_s, sel_v, tab_v, sel_s, tab_s, next_v, next_s,
     loc, zw_s, zw_r, y1_s, y1_r, y2_s, y2_r, ty_s, ty_r, tz_s, tz_r, xs_s, xs_r, co_s, co_r,
     ax_s, ax_r, ac_s, ac_r, ay_s, ay_r, pc_s, pc_r, *t,
 ):
@@ -104,16 +106,23 @@
         return w.at[part, rows, :]
 
     def t_send(s, d, h):
-        if s < T_REACH[d]:
-            cut = pl.ds(h * (SLOTS // CUTS), SLOTS // CUTS)
-            here, there = ((NZ - s) % NZ, NZ - s - 1) if d == 0 else (s, s + 1)
+        cut = pl.ds(h * (SLOTS // CUTS), SLOTS // CUTS)
+        here, there = ((NZ - s) % NZ, NZ - s - 1) if d == 0 else (s, s + 1)
+        if s == T_REACH[d] - 1 and h == CUTS - 1:
+            zz = lax.rem(z + here, NZ)
+            for q in range(8):
+                t[18 + d][q] = t[here][next_s[8 * d + q, y * NZ + zz]]
+            send(t[18 + d], t[16 + d], tz_s.at[d, s * CUTS], tz_r.at[d, s * CUTS], zn[d])
+        elif s < T_REACH[d] - 1:
             src = t[here].at[cut]
             if s == 0:
                 src = tiles.at[cut, pl.ds(pl.multiple_of(PART * i, PART), PART), :]
             send(src, t[there].at[cut], tz_s.at[d, s * CUTS + h], tz_r.at[d, s * CUTS + h], zn[d])
 
     def t_wait(s, d, h):
-        if s < T_REACH[d]:
+        if s == T_REACH[d] - 1 and h == CUTS - 1:
+            arrived(t[16 + d], tz_s.at[d, s * CUTS], tz_r.at[d, s * CUTS], zn[d])
+        elif s < T_REACH[d] - 1:
             cut = pl.ds(h * (SLOTS // CUTS), SLOTS // CUTS)
             arrived(t[NZ - s - 1 if d == 0 else s + 1].at[cut], tz_s.at[d, s * CUTS + h], tz_r.at[d, s * CUTS + h], zn[d])
 
@@ -144,12 +153,13 @@
 
     def y_forward(g):
         for j, zz in group(g):
-            send(w_at(y, zz), w_at(y, zz), y1_s.at[1, j], y1_r.at[1, j], yn[1])
+            send(w_at(y, zz, 1), w_at(y, zz, 1), y1_s.at[1, j], y1_r.at[1, j], yn[1])
             send(w_at(y, zz, 1), w_at(y, zz, 1), y1_s.at[0, j], y1_r.at[0, j], yn[0])
+            send(w_at(y, zz, 0), w_at(y, zz, 0), y1_s.at[2, j], y1_r.at[2, j], yn[1])
 
     def y_relay(g):
         for j, zz in group(g):
-            arrived(w_at(yr, zz), y1_s.at[1, j], y1_r.at[1, j], yn[1])
+            arrived(w_at(yr, zz, 1), y1_s.at[1, j], y1_r.at[1, j], yn[1])
             arrived(w_at(ym, zz, 1), y1_s.at[0, j], y1_r.at[0, j], yn[0])
             e = int(j in RIM_OUT)
             part = w_at(ym if e else yr, zz, 1)
@@ -175,12 +185,16 @@
     slot = iota((SLOTS, 64), 0)
     used = slot < count_v[...]
     owner = lax.shift_right_logical(dest_v[...], 1)
-    for yy in range(NY):
-        hit = used & (owner == yy * NZ + z)
-        first = jnp.min(jnp.where(hit, slot, SLOTS - 1), axis=0, keepdims=True)
-        second = jnp.max(jnp.where(hit, slot, 0), axis=0, keepdims=True)
-        sel_v[2 * yy:2 * yy + 1, :] = jnp.clip(first, 0, SLOTS - 1)
-        sel_v[2 * yy + 1:2 * yy + 2, :] = jnp.clip(second, 0, SLOTS - 1)
+
+    def pick(table, lo, zz):
+        for yy in range(NY):
+            hit = used & (owner == yy * NZ + zz)
+            first = jnp.min(jnp.where(hit, slot, SLOTS - 1), axis=0, keepdims=True)
+            second = jnp.max(jnp.where(hit, slot, 0), axis=0, keepdims=True)
+            table[lo + 2 * yy:lo + 2 * yy + 1, :] = jnp.clip(first, 0, SLOTS - 1)
+            table[lo + 2 * yy + 1:lo + 2 * yy + 2, :] = jnp.clip(second, 0, SLOTS - 1)
+
+    pick(sel_v, 0, z)
     sel_copy = pltpu.make_async_copy(sel_v, sel_s, loc.at[11])
     sel_copy.start()
     local[0].wait()
@@ -201,7 +215,11 @@
                 yy = lax.rem(y + dy, NY)
                 for j in range(2):
                     buf, row = (ysend, dy - 1) if dy else (yrecv, 0)
-                    buf[(row * NZ + span(g)[0] + n) * 2 + j] = t[far[n]][sel_s[2 * yy + j, y * NZ + zz]]
+                    if far[n] in LAST:
+                        tile = t[16 + LAST.index(far[n])][2 * yy + j]
+                    else:
+                        tile = t[far[n]][sel_s[2 * yy + j, y * NZ + zz]]
+                    buf[(row * NZ + span(g)[0] + n) * 2 + j] = tile
         for dy in (1, 3, 2):
             send(y_piece(ysend, dy - 1, g), y_piece(yrecv, dy, g),
                  ty_s.at[dy - 1, g], ty_r.at[dy - 1, g], at(y + dy, z))
@@ -251,17 +269,21 @@
                 arrived(part, xs.at[d, 2], xr.at[d, 2], xn[d])
                 send(part, part, cs.at[6 + d], cr.at[6 + d], twin)
 
-        def finish():
+        def own_in():
             for h in range(2):
                 arrived(piece(other(i), h), cs.at[h], cr.at[h], twin)
+
+        def near_in():
             for n in range(2):
                 for d in range(2):
                     part = piece(other(xn[1 - d][1]), (d + n) % 2)
                     arrived(part, cs.at[2 + 2 * n + d], cr.at[2 + 2 * n + d], twin)
+
+        def last_in():
             for d in range(2):
                 arrived(piece(other(at_x(x + 2)[1]), d), cs.at[6 + d], cr.at[6 + d], twin)
 
-        return start, near, last, finish
+        return start, near, last, own_in, near_in, last_in
 
     am_spread = spread(lambda ii, h: am.at[h, part_rows(ii), :], ax_s, ax_r, ac_s, ac_r)
     half = NCT // 2
@@ -294,24 +316,31 @@
         rows += chain(down, down.T, n)
         for n, line in enumerate(rows):
             tab_v[n:n + 1, :] = jnp.clip(line, 0, 127 if n < 4 else SLOTS - 1)
-        c = pltpu.make_async_copy(tab_v, tab_s, loc.at[12])
-        c.start()
-        return c
-
-    for s in range(steps):
-        for k in range(2):
+        for d in range(2):
+            pick(next_v, 8 * d, lax.rem(z + 1 + (NZ - 2) * d, NZ))
+        out = [pltpu.make_async_copy(tab_v, tab_s, loc.at[12]), pltpu.make_async_copy(next_v, next_s, loc.at[13])]
+        for c in out:
+            c.start()
+        return out
+
+    for s in range(steps + BEHIND):
+        sw = s - BEHIND
+        for h in range(CUTS):
             for d in range(2):
-                t_wait(s, d, k)
-                t_send(s + 1, d, k)
-            for d in range(2):
-                z_wait(s, d, k)
-                z_send(s + 1, d, k)
-        choose(s + 1)
-        y_forward(s + 1)
+                t_wait(s, d, h)
+                t_send(s + 1, d, h)
+            for d in range(2 if h < 2 and sw >= 0 else 0):
+                z_wait(sw, d, h)
+                z_send(sw + 1, d, h)
+        if s < steps:
+            choose(s + 1)
+        if sw >= 0:
+            y_forward(sw + 1)
         if s == 0:
             tab_copy = tables()
         if s == 1:
-            tab_copy.wait()
+            for c in tab_copy:
+                c.wait()
             lax.fori_loop(0, SLOTS, place_slices, jnp.zeros((PART, TILE), F32))
             for r in range(2):
                 for c in range(12):
@@ -330,8 +359,8 @@
             am_spread[1]()
         if s == 7:
             am_spread[2]()
-        if s >= LAG:
-            y_relay(s - LAG)
+        if sw >= LAG:
+            y_relay(sw - LAG)
 
     for g in range(steps + 1):
         for dy in (1, 3, 2):
@@ -352,7 +381,8 @@
     for g in range(steps - LAG, steps + 1):
         y_relay(g)
 
-    am_spread[3]()
+    for take in am_spread[3:]:
+        take()
 
     def wl_rows(yy):
         return w[0, pl.ds(pl.multiple_of(yy * DEPTH, DEPTH), DEPTH), :]
@@ -363,26 +393,32 @@
             add = jnp.dot(left, wl_rows(yy), preferred_element_type=F32)
             acc[...] = acc[...] + add if n else add
 
+    for g in range(steps + 1):
+        for j, zz in group(g):
+            arrived(w_at(yr, zz, 0), y1_s.at[2, j], y1_r.at[2, j], yn[1])
     half_ladder(am, acc_p)
     send(acc_p, from_mate, pc_s.at[0], pc_r.at[0], yn[0])
+    def cycle(xx, fresh=False):
+        xx = lax.rem(xx + NX, NX)
+        left = bt[:, pl.ds(pl.multiple_of(xx * 2 * PART, 2 * PART), 2 * PART), :].reshape(DEPTH, 2 * TILE)
+        right = jnp.concatenate(
+            [w[1, pl.ds(pl.multiple_of(c * TILE + xx * 2 * PART, 2 * PART), 2 * PART), :] for c in range(NCT)], axis=0)
+        add = lax.dot_general(left, right, (((0,), (0,)), ((), ())), preferred_element_type=F32)
+        acc_c[...] = add if fresh else acc_c[...] + add
+
     bt_spread[1]()
-    half_ladder(a, acc_l)
-    bt_spread[2]()
-
-    def cycle(yy, fresh=False):
-        cut = pl.ds(pl.multiple_of(yy * DEPTH, DEPTH), DEPTH)
-        part = bt[pl.ds(yy * (DEPTH // TILE), DEPTH // TILE)].reshape(DEPTH, 2 * TILE)
-        add = lax.dot_general(part, w[1, cut, :], (((0,), (0,)), ((), ())), preferred_element_type=F32)
-        acc_c[...] = add if fresh else acc_c[...] + add
-
-    bt_spread[3]()
-    cycle(y, True)
-    cycle(ym)
-    cycle(yr)
     for g in range(steps + 1):
         for j, zz in group(g):
             arrived(w_at(yf, zz, 1), y2_s.at[j], y2_r.at[j], yn[int(j in RIM_OUT)])
-    cycle(yf)
+    bt_spread[3]()
+    cycle(x, True)
+    half_ladder(a, acc_l)
+    bt_spread[2]()
+    bt_spread[4]()
+    cycle(x + 1)
+    cycle(x - 1)
+    bt_spread[5]()
+    cycle(x + 2)
     out_c[...] = acc_c[...].astype(BF16)
     arrived(from_mate, pc_s.at[0], pc_r.at[0], yn[0])
     out_l[...] = (acc_l[...] + from_mate[...]).astype(BF16)
@@ -421,13 +457,14 @@
             pltpu.SMEM((3, NCT), I32), pltpu.SMEM((3, NCT), I32), pltpu.SMEM((1, 64), I32),
             pltpu.VMEM((8, 64), I32), pltpu.VMEM((8, TILE), I32),
             pltpu.SMEM((8, 64), I32), pltpu.SMEM((8, TILE), I32),
-            dma((13,)),
+            pltpu.VMEM((16, 64), I32), pltpu.SMEM((16, 64), I32),
+            dma((14,)),
             dma((2, 2 * NZ)), dma((2, 2 * NZ)),
-            dma((2, NZ)), dma((2, NZ)), dma((NZ,)), dma((NZ,)),
+            dma((3, NZ)), dma((3, NZ)), dma((NZ,)), dma((NZ,)),
             dma((NY - 1, 9)), dma((NY - 1, 9)), dma((2, 8 * CUTS)), dma((2, 8 * CUTS)),
             dma((2, 3)), dma((2, 3)), dma((8,)), dma((8,)), dma((2, 3)), dma((2, 3)), dma((8,)), dma((8,)),
             dma((1,)), dma((1,)), dma((1,)), dma((1,)),
-            *[pltpu.VMEM((SLOTS, PART, TILE), BF16)] * NZ,
+            *[pltpu.VMEM((SLOTS, PART, TILE), BF16)] * NZ, *[pltpu.VMEM((8, PART, TILE), BF16)] * 4,
         ],
         compiler_params=pltpu.CompilerParams(
             collective_id=0, has_side_effects=True, vmem_limit_bytes=ROOM * 2**20),

time: 70.6 us -> 69.3 us (0.982)
  Pallas kernels: 67.5 us -> 66.2 us
    pallas_call x1, Pallas kernels: 67.5 us -> 66.2 us  [shards(): pl.pallas_call(kernel, out_shape=(out, out), in_specs=[anywhere] * 9, out...]
where the time goes in v4:
time: 69.3 us; the launch traced here: 69.2 us
  Pallas kernels  66.2 us (96%)
  local copies, waits for them, and re-layouts  2.34 us (3%)
    pallas_call x1, Pallas kernels, shards(): pl.pallas_call(kernel, out_shape=(out, out), in_specs=[anywhere] * 9, out...  66.2 us
    unnamed x4, local copies, waits for them, and re-layouts  2.34 us

profile of v4, /device:TPU:1, one launch (start us, length us, event | category | flops | bytes accessed | tf_op | source)
XLA Modules:
  0.0 69.2 jit_solution(2454162117390497100)
XLA Ops:
  0.6 66.2 %shard_map.104 = (bf16[256,384]{1,0:T(8,128)(2,1)}, bf16[256,384]{1,0:T(8,128)(2,1)}) custom-call(s32[24,64]{1,0:T(8,128)} %bitcast.6, s32[24,64]{1,0:T(8,128)} %bitcast.7, s32[24,64]{1,0:T(8,128)} %bitcast.8, s32[1,64]{1,0:T(1,128)} %bitcast.11, s32[3,24]{1,0:T(4,128)} %bitcast.9, s32[3,24]{1,0:T(4,128)} %bitcast.10, bf16[48,384]{1,0:T(8,128)(2,1)} %wl.1, ...), custom_call_target="tpu_custom_call" | custom-call | flops 1300000000 | bytes 3000000 | tf_op jit(solution)/shard_map/pallas_call | solution.py:437
  66.8 0.0 copy-start
  66.8 1.7 %copy.13 = bf16[256,384]{1,0:T(8,128)(2,1)} copy(bf16[256,384]{1,0:T(8,128)(2,1)} %get-tuple-element.4) | data formatting | bytes 393216
  68.5 0.0 copy-done
  68.5 0.7 copy.14
Async XLA Ops:
  66.8 1.7 %copy-start = (bf16[256,384]{1,0:T(8,128)(2,1)S(1)}, bf16[256,384]{1,0:T(8,128)(2,1)}, u32[]{:S(2)}) copy-start(bf16[256,384]{1,0:T(8,128)(2,1)} %get-tuple-element.5) | copy-start | bytes 589828

commit v5 on v4

--- a/solution.py
+++ b/solution.py
@@ -15,7 +15,7 @@
 ROWS = 48
 COLS = 384
 DEPTH = NZ * ROWS
-LAG = 4
+LAG = 5
 W_REACH = (8, 7)
 T_REACH = (7, 8)
 LAST = (NZ - T_REACH[0], T_REACH[1])
@@ -175,7 +175,7 @@
         if s < reach[d]:
             arrived(w_at(y, zz, k), zw_s.at[d, 2 * s + k], zw_r.at[d, 2 * s + k], zn[d])
 
-    for k in range(2):
+    for k in (1, 0):
         for d in range(2):
             z_send(0, d, k)
     y_forward(0)
@@ -329,11 +329,15 @@
             for d in range(2):
                 t_wait(s, d, h)
                 t_send(s + 1, d, h)
-            for d in range(2 if h < 2 and sw >= 0 else 0):
-                z_wait(sw, d, h)
-                z_send(sw + 1, d, h)
+            if h == 0:
+                for d in range(2):
+                    z_wait(sw, d, 1)
+                    z_send(sw + 1, d, 1)
         if s < steps:
             choose(s + 1)
+        for d in range(2):
+            z_wait(sw, d, 0)
+            z_send(sw + 1, d, 0)
         if sw >= 0:
             y_forward(sw + 1)
         if s == 0:

time: 69.3 us -> 68.2 us (0.984)
  Pallas kernels: 66.2 us -> 65.1 us
    pallas_call x1, Pallas kernels: 66.2 us -> 65.1 us  [shards(): pl.pallas_call(kernel, out_shape=(out, out), in_specs=[anywhere] * 9, out...]
where the time goes in v5:
time: 68.2 us; the launch traced here: 68.1 us
  Pallas kernels  65.1 us (95%)
  local copies, waits for them, and re-layouts  2.34 us (3%)
    pallas_call x1, Pallas kernels, shards(): pl.pallas_call(kernel, out_shape=(out, out), in_specs=[anywhere] * 9, out...  65.1 us
    unnamed x4, local copies, waits for them, and re-layouts  2.34 us

profile of v5, /device:TPU:1, one launch (start us, length us, event | category | flops | bytes accessed | tf_op | source)
XLA Modules:
  0.0 68.1 jit_solution(5827197391004967419)
XLA Ops:
  0.6 65.1 %shard_map.104 = (bf16[256,384]{1,0:T(8,128)(2,1)}, bf16[256,384]{1,0:T(8,128)(2,1)}) custom-call(s32[24,64]{1,0:T(8,128)} %bitcast.6, s32[24,64]{1,0:T(8,128)} %bitcast.7, s32[24,64]{1,0:T(8,128)} %bitcast.8, s32[1,64]{1,0:T(1,128)} %bitcast.11, s32[3,24]{1,0:T(4,128)} %bitcast.9, s32[3,24]{1,0:T(4,128)} %bitcast.10, bf16[48,384]{1,0:T(8,128)(2,1)} %wl.1, ...), custom_call_target="tpu_custom_call" | custom-call | flops 1300000000 | bytes 3000000 | tf_op jit(solution)/shard_map/pallas_call | solution.py:441
  65.8 0.0 copy-start
  65.8 1.7 %copy.13 = bf16[256,384]{1,0:T(8,128)(2,1)} copy(bf16[256,384]{1,0:T(8,128)(2,1)} %get-tuple-element.4) | data formatting | bytes 393216
  67.4 0.0 copy-done
  67.4 0.7 copy.14
Async XLA Ops:
  65.8 1.7 %copy-start = (bf16[256,384]{1,0:T(8,128)(2,1)S(1)}, bf16[256,384]{1,0:T(8,128)(2,1)}, u32[]{:S(2)}) copy-start(bf16[256,384]{1,0:T(8,128)(2,1)} %get-tuple-element.5) | copy-start | bytes 589828
